TPU v7x, 128 devices: a whole 4x4x4 slice. The times are simulated.
128 devices in a mesh: slab: 4 (over y_hi, core), filt: 32 (over x, y_lo, z).
Axes of the slice: x: 4, y: 4 (y_hi: 2, y_lo: 2; y = y_hi * 2 + y_lo), z: 4, core: 2. Of those that a mesh axis runs over, the one named last changes fastest.
Arguments:
- volume: float32 [512, 32, 256], P('filt', 'slab'), may hold values from -6 to 6
- filters: float32 [27, 512, 512], P(None, 'filt'), may hold values from -0.0546875 to 0.0546875
- out_grad: float32 [512, 32, 256], P('filt', 'slab'), may hold values from -6 to 6
Outputs:
- activated: float32 [512, 32, 256], P('filt', 'slab')
- input_grad: float32 [512, 32, 256], P('filt', 'slab')
- weight_grad: float32 [27, 512, 512], P(None, 'filt')
All inputs are finite; a program needn't handle non-finite values.
Results may differ from a plain program's by a relative error of at most 0.00012.
Values sent between devices are 32-bit elements; how exact they have to be, the bound alone decides.
A program may use at most 64 MiB of HBM per device.

v0:
```python
import math

import jax
import jax.numpy as jnp
from jax import lax
from jax.sharding import PartitionSpec as P

C = 512
TAPS = 27
HEIGHT = 16
WIDTH = 16


highest = lax.Precision.HIGHEST


def extended_2(block, sides, width):
    for axis, dim in sides:
        count = lax.axis_size(axis)
        forward = [(i, i + 1) for i in range(count - 1)]
        backward = [(target, source) for source, target in forward]
        low = lax.ppermute(
            lax.slice_in_dim(block, block.shape[dim] - width, None, axis=dim), axis, forward
        )
        high = lax.ppermute(lax.slice_in_dim(block, 0, width, axis=dim), axis, backward)
        block = jnp.concatenate([low, block, high], axis=dim)
    return block


def shifted(field, down, across):
    margin = WIDTH + 1
    pads = [(0, 0)] * (field.ndim - 1) + [(margin, margin)]
    padded = jnp.pad(field, pads)
    begin = margin + down * WIDTH + across
    moved = lax.slice_in_dim(padded, begin, begin + HEIGHT * WIDTH, axis=field.ndim - 1)
    column = lax.broadcasted_iota(jnp.int32, (HEIGHT * WIDTH,), 0) % WIDTH + across
    inside = jnp.logical_and(column >= 0, column < WIDTH)
    return jnp.where(inside, moved, 0.0)


def shards(volume, filters, out_grad):
    chan_rows = volume.shape[0]
    depth_rows = volume.shape[1]
    taps_out = filters.shape[0] * filters.shape[1]
    flat_filters = filters.reshape(taps_out, C)
    plane = (depth_rows + 2) * HEIGHT * WIDTH
    extended = extended_2(volume, (("slab", 1),), 1)
    gathered = lax.all_gather(extended, "filt", axis=0, tiled=True).reshape(C, plane)
    responses = jnp.dot(
        flat_filters, gathered, precision=highest, preferred_element_type=jnp.float32
    )
    responses = responses.reshape(TAPS, chan_rows, depth_rows + 2, HEIGHT * WIDTH)
    preact = None
    for index in range(TAPS):
        first = index // 9
        second = index // 3 % 3
        third = index % 3
        term = shifted(responses[index, :, first : first + depth_rows], second - 1, third - 1)
        preact = term if preact is None else preact + term
    positive = jnp.maximum(preact, 0.0)
    activated = positive * positive
    pre_grad = 2.0 * positive * out_grad
    padded_grad = jnp.pad(pre_grad, ((0, 0), (2, 2), (0, 0)))
    stacked = jnp.stack(
        [
            shifted(
                padded_grad[:, 2 - index // 9 : 4 - index // 9 + depth_rows],
                1 - index // 3 % 3,
                1 - index % 3,
            )
            for index in range(TAPS)
        ]
    )
    stacked = stacked.reshape(taps_out, plane)
    local_terms = lax.dot_general(
        stacked,
        gathered,
        (((1,), (1,)), ((), ())),
        precision=highest,
        preferred_element_type=jnp.float32,
    )
    voxels = depth_rows * lax.axis_size("slab") * HEIGHT * WIDTH
    summed_terms = lax.psum(local_terms, "slab")
    weight_grad = (summed_terms / math.sqrt(voxels)).reshape(TAPS, chan_rows, C)
    whole = lax.psum_scatter(
        lax.dot_general(
            flat_filters,
            stacked,
            (((0,), (0,)), ((), ())),
            precision=highest,
            preferred_element_type=jnp.float32,
        ),
        "filt",
        scatter_dimension=0,
        tiled=True,
    )
    whole = whole.reshape(chan_rows, depth_rows + 2, HEIGHT * WIDTH)
    rims = jnp.stack([whole[:, 0], whole[:, depth_rows + 1]], axis=1)
    arrived = extended_2(rims, (("slab", 1),), 1)
    input_grad = whole[:, 1 : depth_rows + 1]
    input_grad = input_grad.at[:, 0].add(arrived[:, 0])
    input_grad = input_grad.at[:, depth_rows - 1].add(arrived[:, 3])
    return (activated, input_grad, weight_grad)


def solution(mesh):
    placed = (P("filt", "slab", None), P(None, "filt", None), P("filt", "slab", None))
    return jax.shard_map(
        shards,
        mesh=mesh,
        in_specs=placed,
        out_specs=(P("filt", "slab", None), P("filt", "slab", None), P(None, "filt", None)),
        check_vma=False,
    )
```

profile of v0, /device:TPU:1, one launch (start us, length us, event | category | flops | bytes accessed | tf_op | source)
XLA Modules:
  0.0 462.8 jit_solution(2461146635068056464)
XLA Ops:
  7.2 1.0 copy.17
  8.3 6.2 %collective-permute-start = (f32[16,1,256]{2,0,1:T(8,128)S(1)}, f32[16,1,256]{2,0,1:T(8,128)S(1)}, u32[]{:S(2)}, u32[]{:S(2)}) collective-permute-start(f32[16,1,256]{2,0,1:T(8,128)S(1)} %get-tuple-element.59), channel_id=1, source_target_pairs={{0,32},{32,64},{64,96},{1,33},{33,65},{65,97},{2,34},{34,66},{66,9... | collective-permute-start | bytes 49160 | tf_op jit(solution)/shard_map/ppermute | solution.py:22
  14.5 1.9 collective-permute-start.1
  16.4 4.6 collective-permute-done.1
  21.0 0.7 pad_maximum_fusion
  21.8 142.1 %all-gather.2.cloned.1.call-done = f32[512,10,256]{2,0,1:T(8,128)} async-done(((f32[16,10,256]{2,0,1:T(8,128)}), f32[512,10,256]{2,0,1:T(8,128)}) %all-gather.2.cloned.1.call-update) | async-done | bytes 5242896 | tf_op jit(solution)/shard_map/all_gather | solution.py:48
  163.9 5.9 %copy.20 = f32[512,10,256]{0,2,1:T(8,128)} copy(f32[512,10,256]{2,0,1:T(8,128)} %all-gather.2.cloned.1.call-done) | data formatting | bytes 10485760 | tf_op jit(solution)/shard_map/all_gather | solution.py:48
  169.8 10.6 %convolution_bitcast_fusion.1 = f32[432,2560]{1,0:T(8,128)} fusion(f32[512,2560]{0,1:T(8,128)} %bitcast.199, f32[432,512]{1,0:T(8,128)S(1)} %bitcast.195), kind=kOutput, calls=%fused_computation.1 | convolution fusion | flops 6794772480 | bytes 10551296 | tf_op jit(solution)/shard_map/dot_general | solution.py:49
  180.5 6.6 %reshape.84 = f32[27,16,10,256]{3,2,1,0:T(8,128)} reshape(f32[432,2560]{1,0:T(8,128)} %convolution_bitcast_fusion.1) | data formatting | bytes 8847360 | tf_op jit(solution)/shard_map/reshape | solution.py:52
  187.1 1.2 slice_bitcast_fusion.25
  188.3 2.6 slice_bitcast_fusion.26
  190.9 2.0 multiply_multiply_fusion
  193.0 0.1 fusion.2
  193.3 0.1 fusion.8
  193.6 0.1 fusion.14
  194.0 0.1 fusion.23
  194.5 0.1 fusion.32
  194.8 0.1 fusion.38
  196.5 4.2 copy.31
  200.7 2.1 copy-done.1
  202.8 10.3 %convolution_bitcast_fusion = f32[512,2560]{0,1:T(8,128)} fusion(f32[432,2560]{1,0:T(8,128)S(1)} %bitcast.197, f32[432,512]{1,0:T(8,128)S(1)} %bitcast.196), kind=kOutput, calls=%fused_computation | convolution fusion | flops 6794772480 | bytes 10551296 | tf_op jit(solution)/shard_map/dot_general | solution.py:86
  213.1 6.0 %copy.25 = f32[512,2560]{1,0:T(8,128)} copy(f32[512,2560]{0,1:T(8,128)} %convolution_bitcast_fusion) | data formatting | bytes 10485760
  219.2 10.8 %fusion.129 = f32[432,512]{1,0:T(8,128)} fusion(f32[432,2560]{1,0:T(8,128)} %bitcast.198, f32[512,2560]{0,1:T(8,128)} %bitcast.200), kind=kOutput, calls=%fused_computation.219 | convolution fusion | flops 6794772480 | bytes 10551296 | tf_op jit(solution)/shard_map/dot_general | solution.py:75
  230.0 0.7 mul.12
  230.6 154.6 %reduce-scatter.4.cloned.1.call-done = f32[16,2560]{1,0:T(8,128)} async-done(((f32[512,2560]{1,0:T(8,128)}), f32[16,2560]{1,0:T(8,128)}) %reduce-scatter.4.cloned.1.call-update) | async-done | bytes 163856
  385.2 1.3 copy.26
  386.7 28.5 %collective-permute-start.2 = (f32[16,1,256]{2,1,0:T(1,128)S(1)}, f32[16,1,256]{2,1,0:T(1,128)S(1)}, u32[]{:S(2)}, u32[]{:S(2)}) collective-permute-start(f32[16,1,256]{2,1,0:T(1,128)S(1)} %copy.29), channel_id=1, source_target_pairs={{0,32},{32,64},{64,96},{1,33},{33,65},{65,97},{2,34},{34,66},{66,9... | collective-permute-start | bytes 49160 | tf_op jit(solution)/shard_map/ppermute | solution.py:22
  415.2 1.9 collective-permute-start.3
  417.1 35.6 %all-reduce.30.cloned.1.call-done = f32[432,512]{1,0:T(8,128)} async-done(((f32[432,512]{1,0:T(8,128)}), f32[432,512]{1,0:T(8,128)}) %all-reduce.30.cloned.1.call-update) | async-done | bytes 884752 | tf_op jit(solution)/shard_map/psum | solution.py:83
  452.7 2.2 broadcast_multiply_fusion
  454.9 0.3 copy.27
  455.6 0.6 copy-done.2
  (49 shorter events, 3.3 us)
Async XLA Ops:
  7.2 162.6 %copy-start = (f32[27,16,512]{2,1,0:T(8,128)S(1)}, f32[27,16,512]{2,1,0:T(8,128)}, u32[]{:S(2)}) copy-start(f32[27,16,512]{2,1,0:T(8,128)} %param.8) | copy-start | bytes 2654212
  7.2 156.7 %all-gather.2.cloned.1.call-start = ((), (), s32[]{:S(2)}) async-start(), calls=%async_computation.1 | async-start | bytes 5406720 | tf_op jit(solution)/shard_map/all_gather | solution.py:48
  8.3 8.2 %collective-permute-start = (f32[16,1,256]{2,0,1:T(8,128)S(1)}, f32[16,1,256]{2,0,1:T(8,128)S(1)}, u32[]{:S(2)}, u32[]{:S(2)}) collective-permute-start(f32[16,1,256]{2,0,1:T(8,128)S(1)} %get-tuple-element.59), channel_id=1, source_target_pairs={{0,32},{32,64},{64,96},{1,33},{33,65},{65,97},{2,34},{34,66},{66,9... | collective-permute-start | bytes 49160 | tf_op jit(solution)/shard_map/ppermute | solution.py:22
  14.5 6.6 %collective-permute-start.1 = (f32[16,1,256]{2,0,1:T(8,128)S(1)}, f32[16,1,256]{2,0,1:T(8,128)S(1)}, u32[]{:S(2)}, u32[]{:S(2)}) collective-permute-start(f32[16,1,256]{2,0,1:T(8,128)S(1)} %get-tuple-element.60), channel_id=1, source_target_pairs={{32,0},{64,32},{96,64},{33,1},{65,33},{97,65},{34,2},{66,34},{98,6... | collective-permute-start | bytes 49160 | tf_op jit(solution)/shard_map/ppermute | solution.py:25
  21.7 363.5 %reduce-scatter.4.cloned.1.call-start = ((), (), s32[]{:S(2)}) async-start(), calls=%async_computation.3 | async-start | bytes 5406720
  180.5 10.4 %copy-start.3 = (f32[16,8,256]{2,1,0:T(8,128)S(1)}, f32[16,8,256]{2,1,0:T(8,128)}, u32[]{:S(2)}) copy-start(f32[16,8,256]{2,1,0:T(8,128)} %param.9) | copy-start | bytes 393220
  200.7 2.1 copy-start.1
  219.1 233.6 %all-reduce.30.cloned.1.call-start = ((), (), s32[]{:S(2)}) async-start(), calls=%async_computation.2 | async-start | bytes 1769472 | tf_op jit(solution)/shard_map/psum | solution.py:83
  386.7 68.6 %collective-permute-start.2 = (f32[16,1,256]{2,1,0:T(1,128)S(1)}, f32[16,1,256]{2,1,0:T(1,128)S(1)}, u32[]{:S(2)}, u32[]{:S(2)}) collective-permute-start(f32[16,1,256]{2,1,0:T(1,128)S(1)} %copy.29), channel_id=1, source_target_pairs={{0,32},{32,64},{64,96},{1,33},{33,65},{65,97},{2,34},{34,66},{66,9... | collective-permute-start | bytes 49160 | tf_op jit(solution)/shard_map/ppermute | solution.py:22
  415.2 40.2 %collective-permute-start.3 = (f32[16,1,256]{2,1,0:T(1,128)S(1)}, f32[16,1,256]{2,1,0:T(1,128)S(1)}, u32[]{:S(2)}, u32[]{:S(2)}) collective-permute-start(f32[16,1,256]{2,1,0:T(1,128)S(1)} %copy.30), channel_id=1, source_target_pairs={{32,0},{64,32},{96,64},{33,1},{65,33},{97,65},{34,2},{66,34},{98,6... | collective-permute-start | bytes 49160 | tf_op jit(solution)/shard_map/ppermute | solution.py:25
  455.6 0.7 copy-start.2
Sparse Core Ops, SparseCore 0:
  21.9 141.9 all-gather.1
  219.2 165.9 reduce-scatter.3
  388.3 64.3 all-reduce.29
where the time goes:
time: 463 us
  waiting for transfers between devices  337 us (73%)
  starting transfers between devices  38.7 us (8%)
  local copies, waits for them, and re-layouts  32.5 us (7%)
  matrix products  31.7 us (7%)
  between operations  14.2 us (3%)
  other arithmetic  8.87 us (2%)
    unnamed x4, waiting for transfers between devices  155 us
    all_gather x1, waiting for transfers between devices, shards(): lax.all_gather(extended, 'filt', axis=0, tiled=True).reshape(C, plane)  142 us
    psum x1, waiting for transfers between devices, shards(): summed_terms = lax.psum(local_terms, 'slab')  35.6 us
    ppermute x2, starting transfers between devices, extended_2(): lax.ppermute(lax.slice_in_dim(block, block.shape[dim] - width, None, axis...  34.7 us
    unnamed x16, local copies, waits for them, and re-layouts  15.8 us
    dot_general x1, matrix products, shards(): lax.dot_general(stacked, gathered, (((1,), (1,)), ((), ())), precision=hi...  10.8 us
    dot_general x1, matrix products, shards(): jnp.dot(flat_filters, gathered, precision=highest, preferred_element_type...  10.6 us
    dot_general x1, matrix products, shards(): lax.dot_general(flat_filters, stacked, (((0,), (0,)), ((), ())), precisio...  10.3 us
  transfers between devices with their start and end apart: 7, of which 4 were waited for; matrix products, arithmetic and copies ran while one was open for 3% of the time, Pallas kernels for 0%

commit v1 on v0

v1 whole, which is shorter than its diff:
```python
import math

import jax
import jax.numpy as jnp
from jax import lax
from jax.experimental import pallas as pl
from jax.experimental.pallas import tpu as pltpu
from jax.sharding import PartitionSpec as P

TAPS = 27
PAD = 28
WIDTH = 16
PLANE = 256
ROWS = 16
PLANES = 8
SLABS = 4
X, GY, GZ = 4, 2, 4

GATHER_CHUNKS = ((0, 2), (6, 2), (2, 2), (4, 2))
REDUCE_CHUNKS = ((0, 2), (2, 2), (4, 2), (6, 2))
INPUT_CHUNKS = ((2, 2), (4, 2), (0, 2), (6, 2))

F32 = jnp.float32
BF16 = jnp.bfloat16


def split(value):
    high = value.astype(BF16)
    low = (value - high.astype(F32)).astype(BF16)
    return high, low


def product(left_high, left_low, right_high, right_low, dims):
    def one(left, right):
        return lax.dot_general(left, right, (dims, ((), ())), preferred_element_type=F32)

    return one(left_high, right_high) + (one(left_high, right_low) + one(left_low, right_high))


def kernel(
    vol, fil, og, act, ig, wg,
    g32, gh, gl, fa, w9h, w9l, wc, wth, wtl, taps, part, prec, pgx, sh, sl,
    wacc, wsum, w1b, w2b, wout, igp, igr,
    gat_s, gat_r, fil_s, fil_r, hal_s, hal_r, rs_s, rs_r, ag_s, ag_r, ph_s, ph_r,
    in_s, in_r, w1_s, w1_r, w2_s, w2_r, w3_s, w3_r, w5_s, w5_r,
):
    G = GY * GZ
    I = ROWS * G
    O = ROWS * X
    s = lax.axis_index("slab")
    f = lax.axis_index("filt")
    x = f // G
    g = f % G
    gy = g // GZ
    gz = g % GZ
    core = s % 2
    half = s // 2
    mate = half * 2 + (1 - core)
    across = (s + 2) % SLABS
    other = (mate + 2) % SLABS

    def along_x(j):
        return (x + j) % X

    group = []
    for dy in range(GY):
        for dz in range(GZ):
            if dy or dz:
                group.append(((gy + dy) % GY) * GZ + (gz + dz) % GZ)

    def rows(index):
        return pl.ds(pl.multiple_of(index * ROWS, ROWS), ROWS)

    barrier = pltpu.get_barrier_semaphore()
    partners = [(s, x * G + to) for to in group]
    partners += [(s, along_x(j) * G + g) for j in range(1, X)]
    partners += [(across, along_x(j) * G + g) for j in range(1, X)]
    partners += [(mate, f), (across, f), (other, f)]
    for partner in partners:
        pl.semaphore_signal(
            barrier, inc=1, device_id=partner, device_id_type=pl.DeviceIdType.MESH
        )

    for d in range(PLANES):
        g32[1 + d, rows(g), :] = vol[:, d, :]

    pl.semaphore_wait(barrier, len(partners))

    def remote(src, dst, send, recv, device):
        return pltpu.make_async_remote_copy(
            src_ref=src, dst_ref=dst, send_sem=send, recv_sem=recv,
            device_id=device, device_id_type=pl.DeviceIdType.MESH,
        )

    sent = []

    gather = {}
    for n, (d, w) in enumerate(GATHER_CHUNKS):
        for j, to in enumerate(group):
            here = g32.at[pl.ds(1 + d, w), rows(g), :]
            copy = remote(here, here, gat_s.at[n, j], gat_r.at[n, j], (s, x * G + to))
            copy.start()
            gather.setdefault(n, []).append(copy)
            sent.append(copy)
    filters = []
    for j in range(1, X):
        to = along_x(j)
        copy = remote(
            fil.at[:, :, pl.ds(pl.multiple_of(to * I, I), I)], fa.at[x],
            fil_s.at[j - 1], fil_r.at[j - 1], (s, to * G + g),
        )
        copy.start()
        filters.append(copy)
        sent.append(copy)
    fa[x] = fil[:, :, pl.ds(pl.multiple_of(x * I, I), I)]

    @pl.when(s == 0)
    def _():
        g32[0] = jnp.zeros((I, PLANE), F32)
        pgx[0] = jnp.zeros((O, PLANE), F32)

    @pl.when(s == SLABS - 1)
    def _():
        g32[PLANES + 1] = jnp.zeros((I, PLANE), F32)
        pgx[PLANES + 1] = jnp.zeros((O, PLANE), F32)

    wsum[:, TAPS] = jnp.zeros((X, ROWS, I), F32)
    wc[TAPS * O :] = jnp.zeros((wc.shape[0] - TAPS * O, I), F32)

    for copy in filters:
        copy.wait_recv()
    for a in range(3):
        for k in range(9):
            block = fa[:, 9 * a + k].reshape(O, I)
            high, low = split(block)
            w9h[k * O : (k + 1) * O, a * I : (a + 1) * I] = high
            w9l[k * O : (k + 1) * O, a * I : (a + 1) * I] = low
            wc[((2 - a) * 9 + k) * O : ((2 - a) * 9 + k + 1) * O, :] = block

    def transpose(n, carry):
        start = pl.multiple_of(n * 128, 128)
        high, low = split(wc[pl.ds(start, 128), :].T)
        wth[:, pl.ds(start, 128)] = high
        wtl[:, pl.ds(start, 128)] = low
        return carry

    lax.fori_loop(0, wc.shape[0] // 128, transpose, 0)

    def neighbours(buffer, send, recv):
        up = remote(
            buffer.at[PLANES], buffer.at[0], send.at[0], recv.at[0], ((s + 1) % SLABS, f)
        )
        down = remote(
            buffer.at[1], buffer.at[PLANES + 1], send.at[1], recv.at[1], ((s + 3) % SLABS, f)
        )

        def start():
            @pl.when(s < SLABS - 1)
            def _():
                up.start()

            @pl.when(s > 0)
            def _():
                down.start()

        def arrive():
            @pl.when(s > 0)
            def _():
                up.wait_recv()

            @pl.when(s < SLABS - 1)
            def _():
                down.wait_recv()

        def leave():
            @pl.when(s < SLABS - 1)
            def _():
                up.wait_send()

            @pl.when(s > 0)
            def _():
                down.wait_send()

        return start, arrive, leave

    edge_start, edge_arrive, edge_leave = neighbours(g32, hal_s, hal_r)
    rim_start, rim_arrive, rim_leave = neighbours(pgx, ph_s, ph_r)

    def halve(e, carry):
        high, low = split(g32[e])
        gh[e] = high
        gl[e] = low
        return carry

    for n in range(len(GATHER_CHUNKS)):
        for copy in gather[n]:
            copy.wait_recv()
        if n == 1:
            edge_start()
    lax.fori_loop(1, PLANES + 1, halve, 0)
    edge_arrive()
    halve(0, 0)
    halve(PLANES + 1, 0)

    lane = lax.broadcasted_iota(jnp.int32, (O, PLANE), 1)
    column = lane % WIDTH
    not_left = column >= 1
    not_right = column <= WIDTH - 2
    not_top = lane >= WIDTH
    not_bottom = lane < PLANE - WIDTH

    def forward(d, carry):
        right_high = gh[pl.ds(d, 3)].reshape(3 * I, PLANE)
        right_low = gl[pl.ds(d, 3)].reshape(3 * I, PLANE)
        taps[...] = product(w9h[...], w9l[...], right_high, right_low, ((1,), (0,)))

        def line(b):
            def tap(c):
                k = 3 * b + c
                return taps[k * O : (k + 1) * O, :]

            total = tap(1)
            total += jnp.where(not_left, pltpu.roll(tap(0), 1, 1), 0.0)
            total += jnp.where(not_right, pltpu.roll(tap(2), PLANE - 1, 1), 0.0)
            return total

        total = line(1)
        total += jnp.where(not_top, pltpu.roll(line(0), WIDTH, 1), 0.0)
        total += jnp.where(not_bottom, pltpu.roll(line(2), PLANE - WIDTH, 1), 0.0)
        part[d] = total
        return carry

    reduce = []
    for n, (d, w) in enumerate(REDUCE_CHUNKS):
        lax.fori_loop(d, d + w, forward, 0)
        copies = []
        for j in range(1, X):
            to = along_x(j)
            copy = remote(
                part.at[pl.ds(d, w), rows(to), :], prec.at[j - 1, pl.ds(d, w)],
                rs_s.at[n, j - 1], rs_r.at[n, j - 1], (s, to * G + g),
            )
            copy.start()
            copies.append(copy)
            sent.append(copy)
        reduce.append(copies)

    spread = []
    for n, (d, w) in enumerate(REDUCE_CHUNKS):
        for copy in reduce[n]:
            copy.wait_recv()
        for e in range(d, d + w):
            total = part[e, rows(x), :]
            for j in range(X - 1):
                total += prec[j, e]
            positive = jnp.maximum(total, 0.0)
            act[:, e, :] = positive * positive
            pgx[1 + e, rows(x), :] = 2.0 * positive * og[:, e, :]
        copies = []
        for j in range(1, X):
            here = pgx.at[pl.ds(1 + d, w), rows(x), :]
            copy = remote(
                here, here, ag_s.at[n, j - 1], ag_r.at[n, j - 1], (s, along_x(j) * G + g)
            )
            copy.start()
            copies.append(copy)
            sent.append(copy)
        spread.append(copies)

    def stack(e, carry):
        field = pgx[e]
        for b in range(3):
            if b == 0:
                moved = jnp.where(not_bottom, pltpu.roll(field, PLANE - WIDTH, 1), 0.0)
            elif b == 1:
                moved = field
            else:
                moved = jnp.where(not_top, pltpu.roll(field, WIDTH, 1), 0.0)
            for c in range(3):
                if c == 0:
                    last = jnp.where(not_right, pltpu.roll(moved, PLANE - 1, 1), 0.0)
                elif c == 1:
                    last = moved
                else:
                    last = jnp.where(not_left, pltpu.roll(moved, 1, 1), 0.0)
                k = 3 * b + c
                high, low = split(last)
                sh[e, k * O : (k + 1) * O, :] = high
                sl[e, k * O : (k + 1) * O, :] = low
        return carry

    def weigh(d, carry):
        stack(d + 1, 0)
        term = product(
            sh[d + 1], sl[d + 1],
            gh[pl.ds(d, 3)].reshape(3 * I, PLANE), gl[pl.ds(d, 3)].reshape(3 * I, PLANE),
            ((1,), (1,)),
        )
        wacc[...] += term
        return carry

    wacc[...] = jnp.zeros_like(wacc)
    for n, (d, w) in enumerate(REDUCE_CHUNKS):
        for copy in spread[n]:
            copy.wait_recv()
        lax.fori_loop(d, d + w, weigh, 0)
    rim_start()

    for a in range(3):
        for k in range(9):
            block = wacc[k * O : (k + 1) * O, a * I : (a + 1) * I]
            wsum[:, 9 * a + k] = block.reshape(X, ROWS, I)

    H = PAD // 2
    Q = PAD // 4
    near = core * H
    quarter = near + half * Q
    first = remote(
        wsum.at[:, pl.ds((1 - core) * H, H)], w1b, w1_s, w1_r, (mate, f)
    )
    first.start()
    sent.append(first)

    def backward(d, carry):
        igp[d] = product(
            wth[:, : TAPS * O], wtl[:, : TAPS * O],
            sh[pl.ds(d, 3)].reshape(TAPS * O, PLANE), sl[pl.ds(d, 3)].reshape(TAPS * O, PLANE),
            ((1,), (0,)),
        )
        return carry

    inward = []

    def input_chunk(n):
        d, w = INPUT_CHUNKS[n]
        lax.fori_loop(d, d + w, backward, 0)
        copies = []
        for j, to in enumerate(group):
            copy = remote(
                igp.at[pl.ds(d, w), rows(to), :], igr.at[j, pl.ds(d, w)],
                in_s.at[n, j], in_r.at[n, j], (s, x * G + to),
            )
            copy.start()
            copies.append(copy)
            sent.append(copy)
        inward.append(copies)

    input_chunk(0)

    first.wait_recv()
    wsum[:, pl.ds(near, H)] += w1b[...]
    second = remote(
        wsum.at[:, pl.ds(near + (1 - half) * Q, Q)], w2b, w2_s, w2_r, (across, f)
    )
    second.start()
    sent.append(second)

    input_chunk(1)
    rim_arrive()
    stack(0, 0)
    stack(PLANES + 1, 0)
    input_chunk(2)

    scale = 1.0 / math.sqrt(PLANES * SLABS * PLANE)
    second.wait_recv()
    wsum[:, pl.ds(quarter, Q)] = (wsum[:, pl.ds(quarter, Q)] + w2b[...]) * scale
    third = []
    lanes = pl.ds(pl.multiple_of(x * I, I), I)
    for j in range(X):
        to = along_x(j)
        for k, slab in enumerate((s, across)):
            if j == 0 and k == 0:
                continue
            copy = remote(
                wsum.at[to, pl.ds(quarter, Q)], wout.at[pl.ds(quarter, Q), :, lanes],
                w3_s.at[j, k], w3_r.at[j, k], (slab, to * G + g),
            )
            copy.start()
            third.append(copy)
            sent.append(copy)
    wout[pl.ds(quarter, Q), :, lanes] = wsum[x, pl.ds(quarter, Q)]

    input_chunk(3)

    for copy in third:
        copy.wait_recv()
    here = wout.at[pl.ds(near, H)]
    last = remote(here, here, w5_s, w5_r, (mate, f))
    last.start()
    sent.append(last)

    for n, (d, w) in enumerate(INPUT_CHUNKS):
        for copy in inward[n]:
            copy.wait_recv()
        for e in range(d, d + w):
            total = igp[e, rows(g), :]
            for j in range(G - 1):
                total += igr[j, e]
            ig[:, e, :] = total

    last.wait_recv()
    wg[...] = wout[:TAPS]

    for copy in sent:
        copy.wait_send()
    edge_leave()
    rim_leave()


def scratch():
    G = GY * GZ
    I = ROWS * G
    O = ROWS * X
    columns = -(-TAPS * O // 128) * 128
    vmem = pltpu.VMEM
    dma = pltpu.SemaphoreType.DMA
    return [
        vmem((PLANES + 2, I, PLANE), F32),
        vmem((PLANES + 2, I, PLANE), BF16),
        vmem((PLANES + 2, I, PLANE), BF16),
        vmem((X, TAPS, ROWS, I), F32),
        vmem((9 * O, 3 * I), BF16),
        vmem((9 * O, 3 * I), BF16),
        vmem((columns, I), F32),
        vmem((I, columns), BF16),
        vmem((I, columns), BF16),
        vmem((9 * O, PLANE), F32),
        vmem((PLANES, O, PLANE), F32),
        vmem((X - 1, PLANES, ROWS, PLANE), F32),
        vmem((PLANES + 2, O, PLANE), F32),
        vmem((PLANES + 2, 9 * O, PLANE), BF16),
        vmem((PLANES + 2, 9 * O, PLANE), BF16),
        vmem((9 * O, 3 * I), F32),
        vmem((X, PAD, ROWS, I), F32),
        vmem((X, PAD // 2, ROWS, I), F32),
        vmem((X, PAD // 4, ROWS, I), F32),
        vmem((PAD, ROWS, X * I), F32),
        vmem((PLANES, I, PLANE), F32),
        vmem((G - 1, PLANES, ROWS, PLANE), F32),
        dma((len(GATHER_CHUNKS), G - 1)), dma((len(GATHER_CHUNKS), G - 1)),
        dma((X - 1,)), dma((X - 1,)),
        dma((2,)), dma((2,)),
        dma((len(REDUCE_CHUNKS), X - 1)), dma((len(REDUCE_CHUNKS), X - 1)),
        dma((len(REDUCE_CHUNKS), X - 1)), dma((len(REDUCE_CHUNKS), X - 1)),
        dma((2,)), dma((2,)),
        dma((len(INPUT_CHUNKS), G - 1)), dma((len(INPUT_CHUNKS), G - 1)),
        dma, dma, dma, dma,
        dma((X, 2)), dma((X, 2)),
        dma, dma,
    ]


def shards(volume, filters, out_grad):
    whole = pl.BlockSpec(memory_space=pltpu.VMEM)
    return pl.pallas_call(
        kernel,
        out_shape=(
            jax.ShapeDtypeStruct(volume.shape, F32),
            jax.ShapeDtypeStruct(volume.shape, F32),
            jax.ShapeDtypeStruct(filters.shape, F32),
        ),
        in_specs=[whole] * 3,
        out_specs=(whole,) * 3,
        scratch_shapes=scratch(),
        compiler_params=pltpu.CompilerParams(
            collective_id=0, has_side_effects=True, vmem_limit_bytes=56 * 2**20
        ),
    )(volume, filters, out_grad)


def solution(mesh):
    placed = (P("filt", "slab", None), P(None, "filt", None), P("filt", "slab", None))
    return jax.shard_map(
        shards,
        mesh=mesh,
        in_specs=placed,
        out_specs=(P("filt", "slab", None), P("filt", "slab", None), P(None, "filt", None)),
        check_vma=False,
    )
```

time: 463 us -> 76.5 us (0.17)
  waiting for transfers between devices: 337 us -> 0 us
  Pallas kernels: 0 us -> 71.2 us
  starting transfers between devices: 38.7 us -> 0 us
  matrix products: 31.7 us -> 0 us
  local copies, waits for them, and re-layouts: 32.5 us -> 4.44 us
  between operations: 14.2 us -> 0.65 us
  other arithmetic: 8.87 us -> 0 us
    unnamed x4 -> x0, waiting for transfers between devices: 155 us -> none
    all_gather x1 -> x0, waiting for transfers between devices: 142 us -> none  [shards(): lax.all_gather(extended, 'filt', axis=0, tiled=True).reshape(C, plane)]
    pallas_call x0 -> x1, Pallas kernels: none -> 71.2 us  [shards(): pl.pallas_call(kernel, out_shape=(jax.ShapeDtypeStruct(volume.shape, F32)...]
    ppermute x4 -> x0, starting transfers between devices: 38.6 us -> none  [the longest x2 34.7 us: extended_2(): lax.ppermute(lax.slice_in_dim(block, block.shape[dim] - width, None, axis...]
    psum x1 -> x0, waiting for transfers between devices: 35.6 us -> none  [shards(): summed_terms = lax.psum(local_terms, 'slab')]
    dot_general x3 -> x0, matrix products: 31.7 us -> none  [the longest x1 10.8 us: shards(): lax.dot_general(stacked, gathered, (((1,), (1,)), ((), ())), precision=hi...]
    unnamed x16 -> x5, local copies, waits for them, and re-layouts: 15.8 us -> 4.44 us
    reshape x1 -> x0, local copies, waits for them, and re-layouts: 6.63 us -> none  [shards(): responses.reshape(TAPS, chan_rows, depth_rows + 2, HEIGHT * WIDTH)]
  transfers between devices with their start and end apart: 7 -> 0, of which waited for: 4 -> 0; matrix products, arithmetic and copies ran while one was open for 3% -> 0% of each run, Pallas kernels for 0% -> 0%
where the time goes in v1:
time: 76.5 us; the launch traced here: 76.3 us
  Pallas kernels  71.2 us (93%)
  local copies, waits for them, and re-layouts  4.44 us (6%)
    pallas_call x1, Pallas kernels, shards(): pl.pallas_call(kernel, out_shape=(jax.ShapeDtypeStruct(volume.shape, F32)...  71.2 us
    unnamed x5, local copies, waits for them, and re-layouts  4.44 us

profile of v1, /device:TPU:1, one launch (start us, length us, event | category | flops | bytes accessed | tf_op | source)
XLA Modules:
  0.0 76.3 jit_solution(1456478881440783410)
XLA Ops:
  0.6 71.2 %shard_map.58 = (f32[16,8,256]{2,1,0:T(8,128)}, f32[16,8,256]{2,1,0:T(8,128)}, f32[27,16,512]{2,1,0:T(8,128)}) custom-call(f32[16,8,256]{2,1,0:T(8,128)} %vol.1, f32[27,16,512]{2,1,0:T(8,128)} %fil.1, f32[16,8,256]{2,1,0:T(8,128)} %og.1), custom_call_target="tpu_custom_call" | custom-call | tf_op jit(solution)/shard_map/pallas_call | solution.py:455
  71.8 0.0 copy-start
  71.8 1.6 %copy.9 = f32[16,8,256]{2,1,0:T(8,128)} copy(f32[16,8,256]{2,1,0:T(8,128)} %get-tuple-element.6) | data formatting | bytes 262144
  73.4 0.0 copy-done
  73.4 0.7 copy.10
  74.1 2.2 %copy.11 = f32[27,16,512]{2,1,0:T(8,128)} copy(f32[27,16,512]{2,1,0:T(8,128)} %get-tuple-element.8) | data formatting | bytes 1769472
Async XLA Ops:
  71.8 1.6 %copy-start = (f32[16,8,256]{2,1,0:T(8,128)S(1)}, f32[16,8,256]{2,1,0:T(8,128)}, u32[]{:S(2)}) copy-start(f32[16,8,256]{2,1,0:T(8,128)} %get-tuple-element.7) | copy-start | bytes 393220

commit v2 on v1

v2 whole, which is shorter than its diff:
```python
import math

import jax
import jax.numpy as jnp
from jax import lax
from jax.experimental import pallas as pl
from jax.experimental.pallas import tpu as pltpu
from jax.sharding import PartitionSpec as P

TAPS = 27
PAD = 28
WIDTH = 16
PLANE = 256
ROWS = 16
PLANES = 8
SLABS = 4
X, GY, GZ = 4, 2, 4
G = GY * GZ

GATHER_CHUNKS = ((0, 2, 1), (6, 2, -1), (2, 2, 1), (4, 2, -1))
REDUCE_CHUNKS = ((0, 2, 1), (2, 2, -1), (4, 2, 1), (6, 2, -1))
INPUT_CHUNKS = ((2, 2, 1), (4, 2, -1), (0, 2, 1), (6, 2, -1))
TAP_CHUNKS = ((0, 4, 1), (7, 4, -1), (4, 3, 1), (11, 3, -1))

F32 = jnp.float32
BF16 = jnp.bfloat16


def split(value):
    high = value.astype(BF16)
    low = (value - high.astype(F32)).astype(BF16)
    return high, low


def product(left_high, left_low, right_high, right_low, dims):
    def one(left, right):
        return lax.dot_general(left, right, (dims, ((), ())), preferred_element_type=F32)

    return one(left_high, right_high) + (one(left_high, right_low) + one(left_low, right_high))


def kernel(
    vol, fil, og, act, ig, wg,
    volv, ogv, actv, igv,
    g32, gh, gl, fa, w9h, w9l, wc, wth, wtl, taps, part, prec, pgx, sh, sl,
    wacc, wsum, w1b, wrel, warr, wtot, wout, igp, zrel, zrec, yrec,
    local, g_s, g_r, fil_s, fil_r, hal_s, hal_r, rs_s, rs_r, ag_s, ag_r, ph_s, ph_r,
    in_s, in_r, w1_s, w1_r, wy_s, wy_r, wx_s, wx_r, w5_s, w5_r,
):
    I = ROWS * G
    O = ROWS * X
    H = PAD // 2
    s = lax.axis_index("slab")
    f = lax.axis_index("filt")
    x = f // G
    g = f % G
    gy = g // GZ
    gz = g % GZ
    core = s % 2
    half = s // 2
    mate = half * 2 + (1 - core)
    across = (s + 2) % SLABS
    other = (mate + 2) % SLABS

    def x_of(j):
        return (x + j + X) % X

    def z_of(j):
        return (gz + j + GZ) % GZ

    def at_x(j):
        return (s, x_of(j) * G + g)

    def at_z(j):
        return (s, x * G + gy * GZ + z_of(j))

    flipped = x * G + (1 - gy) * GZ + gz
    at_y = (s, flipped)
    next_y = (((half + gy) % 2) * 2 + core, flipped)
    prev_y = (((half + 1 - gy) % 2) * 2 + core, flipped)

    def rows(index):
        return pl.ds(pl.multiple_of(index * ROWS, ROWS), ROWS)

    def lanes(index):
        return pl.ds(pl.multiple_of(index * I, I), I)

    barrier = pltpu.get_barrier_semaphore()
    partners = [
        (mate, f), at_y, at_z(1), at_z(-1), at_x(1), at_x(-1), at_x(2), (other, f),
        (across, flipped),
    ]
    for partner in partners:
        pl.semaphore_signal(
            barrier, inc=1, device_id=partner, device_id_type=pl.DeviceIdType.MESH
        )

    bring_vol = pltpu.make_async_copy(vol, volv, local.at[0])
    bring_og = pltpu.make_async_copy(og, ogv, local.at[1])
    bring_fil = pltpu.make_async_copy(fil.at[:, :, lanes(x)], fa.at[x], local.at[2])
    bring_vol.start()
    bring_og.start()
    bring_fil.start()

    @pl.when(s == 0)
    def _():
        g32[0] = jnp.zeros((GY, GZ * ROWS, PLANE), F32)
        pgx[0] = jnp.zeros((O, PLANE), F32)

    @pl.when(s == SLABS - 1)
    def _():
        g32[PLANES + 1] = jnp.zeros((GY, GZ * ROWS, PLANE), F32)
        pgx[PLANES + 1] = jnp.zeros((O, PLANE), F32)

    wsum[:, TAPS] = jnp.zeros((X, ROWS, I), F32)
    wc[TAPS * O :] = jnp.zeros((wc.shape[0] - TAPS * O, I), F32)
    wacc[...] = jnp.zeros_like(wacc)

    bring_vol.wait()
    for d in range(PLANES):
        g32[1 + d, gy, rows(gz), :] = volv[:, d, :]

    pl.semaphore_wait(barrier, len(partners))

    sent = []
    leaves = []

    def remote(src, dst, send, recv, device):
        return pltpu.make_async_remote_copy(
            src_ref=src, dst_ref=dst, send_sem=send, recv_sem=recv,
            device_id=device, device_id_type=pl.DeviceIdType.MESH,
        )

    def push(src, dst, sems, index, device):
        send, recv = sems
        copy = remote(src, dst, send.at[index], recv.at[index], device)
        copy.start()
        sent.append(copy)
        return copy


    strip = pl.ds(pl.multiple_of(core * (ROWS // 2), ROWS // 2), ROWS // 2)
    fil_sems = (fil_s, fil_r)
    filters = []
    for j in (1, 3, 2):
        filters.append(
            (
                x_of(-j),
                push(
                    fil.at[:, strip, lanes(x_of(j))], fa.at[x, :, strip], fil_sems, j - 1, at_x(j)
                ),
            )
        )
    g_sems = (g_s, g_r)
    gather = []
    for n, (d, w, way) in enumerate(GATHER_CHUNKS):
        here = g32.at[pl.ds(1 + d, w), gy, rows(gz), :]
        gather.append(
            {
                "y": push(here, here, g_sems, (n, 0), at_y),
                ("own", 1): push(here, here, g_sems, (n, 1), at_z(1)),
                ("own", -1): push(here, here, g_sems, (n, 2), at_z(-1)),
            }
        )
    for n, (d, w, way) in enumerate(GATHER_CHUNKS):
        gather[n]["y"].wait_recv()
        here = g32.at[pl.ds(1 + d, w), 1 - gy, rows(gz), :]
        gather[n]["pair", 1] = push(here, here, g_sems, (n, 3), at_z(1))
        gather[n]["pair", -1] = push(here, here, g_sems, (n, 4), at_z(-1))
    for n, (d, w, way) in enumerate(GATHER_CHUNKS):
        gather[n]["own", way].wait_recv()
        gather[n]["pair", way].wait_recv()
        here = g32.at[pl.ds(1 + d, w), :, rows(z_of(-way)), :]
        gather[n]["far"] = push(here, here, g_sems, (n, 5), at_z(way))

    swaps = []
    for n, (source, copy) in enumerate(filters):
        copy.wait_recv()
        here = fa.at[source, :, strip]
        swaps.append(push(here, here, fil_sems, 3 + n, (mate, f)))
    bring_fil.wait()
    for copy in swaps:
        copy.wait_recv()

    for a in range(3):
        for k in range(9):
            block = fa[:, 9 * a + k].reshape(O, I)
            high, low = split(block)
            w9h[k * O : (k + 1) * O, a * I : (a + 1) * I] = high
            w9l[k * O : (k + 1) * O, a * I : (a + 1) * I] = low
            wc[((2 - a) * 9 + k) * O : ((2 - a) * 9 + k + 1) * O, :] = block

    def transpose(n, carry):
        start = pl.multiple_of(n * 128, 128)
        high, low = split(wc[pl.ds(start, 128), :].T)
        wth[:, pl.ds(start, 128)] = high
        wtl[:, pl.ds(start, 128)] = low
        return carry

    def neighbours(buffer, send, recv):
        up = remote(
            buffer.at[PLANES], buffer.at[0], send.at[0], recv.at[0], ((s + 1) % SLABS, f)
        )
        down = remote(
            buffer.at[1], buffer.at[PLANES + 1], send.at[1], recv.at[1], ((s + 3) % SLABS, f)
        )

        def start():
            @pl.when(s < SLABS - 1)
            def _():
                up.start()

            @pl.when(s > 0)
            def _():
                down.start()

        def arrive():
            @pl.when(s > 0)
            def _():
                up.wait_recv()

            @pl.when(s < SLABS - 1)
            def _():
                down.wait_recv()

        def leave():
            @pl.when(s < SLABS - 1)
            def _():
                up.wait_send()

            @pl.when(s > 0)
            def _():
                down.wait_send()

        return start, arrive, leave

    edge_start, edge_arrive, edge_leave = neighbours(g32, hal_s, hal_r)

    def halve(e, carry):
        high, low = split(g32[e].reshape(I, PLANE))
        gh[e] = high
        gl[e] = low
        return carry

    for n, (d, w, way) in enumerate(GATHER_CHUNKS):
        gather[n]["own", -way].wait_recv()
        gather[n]["pair", -way].wait_recv()
        gather[n]["far"].wait_recv()
        if n == 1:
            edge_start()
            leaves.append(edge_leave)
    lax.fori_loop(1, PLANES + 1, halve, 0)

    lane = lax.broadcasted_iota(jnp.int32, (O, PLANE), 1)
    column = lane % WIDTH
    not_left = column >= 1
    not_right = column <= WIDTH - 2
    not_top = lane >= WIDTH
    not_bottom = lane < PLANE - WIDTH

    def forward(d, carry):
        right_high = gh[pl.ds(d, 3)].reshape(3 * I, PLANE)
        right_low = gl[pl.ds(d, 3)].reshape(3 * I, PLANE)
        taps[...] = product(w9h[...], w9l[...], right_high, right_low, ((1,), (0,)))

        def line(b):
            def tap(c):
                k = 3 * b + c
                return taps[k * O : (k + 1) * O, :]

            total = tap(1)
            total += jnp.where(not_left, pltpu.roll(tap(0), 1, 1), 0.0)
            total += jnp.where(not_right, pltpu.roll(tap(2), PLANE - 1, 1), 0.0)
            return total

        total = line(1)
        total += jnp.where(not_top, pltpu.roll(line(0), WIDTH, 1), 0.0)
        total += jnp.where(not_bottom, pltpu.roll(line(2), PLANE - WIDTH, 1), 0.0)
        part[d] = total
        return carry

    rs_sems = (rs_s, rs_r)
    reduce = []

    def reduce_start(n):
        d, w, way = REDUCE_CHUNKS[n]
        planes = pl.ds(d, w)
        reduce.append(
            [
                push(
                    part.at[planes, rows(x_of(j)), :], prec.at[j - 1, planes],
                    rs_sems, (n, j - 1), at_x(j),
                )
                for j in (2, 1, 3)
            ]
        )

    ag_sems = (ag_s, ag_r)
    spread = []

    def activate(n):
        d, w, way = REDUCE_CHUNKS[n]
        for copy in reduce[n]:
            copy.wait_recv()
        for e in range(d, d + w):
            total = part[e, rows(x), :] + prec[0, e] + (prec[1, e] + prec[2, e])
            positive = jnp.maximum(total, 0.0)
            actv[:, e, :] = positive * positive
            pgx[1 + e, rows(x), :] = 2.0 * positive * ogv[:, e, :]
        here = pgx.at[pl.ds(1 + d, w), rows(x), :]
        spread.append([push(here, here, ag_sems, (n, j - 1), at_x(j)) for j in (2, 1, 3)])

    edge_arrive()
    halve(0, 0)
    halve(PLANES + 1, 0)
    for n, (d, w, way) in enumerate(REDUCE_CHUNKS):
        lax.fori_loop(d, d + w, forward, 0)
        reduce_start(n)
        if n == 1:
            bring_og.wait()
        if n > 1:
            activate(n - 2)
    lax.fori_loop(0, wc.shape[0] // 128, transpose, 0)
    activate(2)
    activate(3)
    give_act = pltpu.make_async_copy(actv, act, local.at[0])
    give_act.start()

    def stack(e, carry):
        field = pgx[e]
        for b in range(3):
            if b == 0:
                moved = jnp.where(not_bottom, pltpu.roll(field, PLANE - WIDTH, 1), 0.0)
            elif b == 1:
                moved = field
            else:
                moved = jnp.where(not_top, pltpu.roll(field, WIDTH, 1), 0.0)
            for c in range(3):
                if c == 0:
                    last = jnp.where(not_right, pltpu.roll(moved, PLANE - 1, 1), 0.0)
                elif c == 1:
                    last = moved
                else:
                    last = jnp.where(not_left, pltpu.roll(moved, 1, 1), 0.0)
                k = 3 * b + c
                high, low = split(last)
                sh[e, k * O : (k + 1) * O, :] = high
                sl[e, k * O : (k + 1) * O, :] = low
        return carry

    def weigh(d, carry):
        stack(d + 1, 0)
        term = product(
            sh[d + 1], sl[d + 1],
            gh[pl.ds(d, 3)].reshape(3 * I, PLANE), gl[pl.ds(d, 3)].reshape(3 * I, PLANE),
            ((1,), (1,)),
        )
        wacc[...] += term
        return carry

    rim_start, rim_arrive, rim_leave = neighbours(pgx, ph_s, ph_r)
    for n, (d, w, way) in enumerate(REDUCE_CHUNKS):
        for copy in spread[n]:
            copy.wait_recv()
        if n == 3:
            rim_start()
            leaves.append(rim_leave)
        lax.fori_loop(d, d + w, weigh, 0)

    for a in range(3):
        for k in range(9):
            block = wacc[k * O : (k + 1) * O, a * I : (a + 1) * I]
            wsum[:, 9 * a + k] = block.reshape(X, ROWS, I)

    near = core * H
    first = push(
        wsum.at[:, pl.ds((1 - core) * H, H)], w1b, (w1_s, w1_r), 0, (mate, f)
    )

    def backward(d, carry):
        value = product(
            wth[:, : TAPS * O], wtl[:, : TAPS * O],
            sh[pl.ds(d, 3)].reshape(TAPS * O, PLANE), sl[pl.ds(d, 3)].reshape(TAPS * O, PLANE),
            ((1,), (0,)),
        )
        igp[d] = value.reshape(GY, GZ * ROWS, PLANE)
        return carry

    in_sems = (in_s, in_r)
    inward = []

    def input_start(n):
        d, w, way = INPUT_CHUNKS[n]
        planes = pl.ds(d, w)
        lax.fori_loop(d, d + w, backward, 0)
        inward.append(
            {
                "far": push(
                    igp.at[planes, :, rows(z_of(2)), :], zrel.at[planes],
                    in_sems, (n, 0), at_z(way),
                ),
                "back": push(
                    igp.at[planes, :, rows(z_of(-way)), :], zrec.at[1, planes],
                    in_sems, (n, 1), at_z(-way),
                ),
            }
        )

    def input_relay(n):
        d, w, way = INPUT_CHUNKS[n]
        planes = pl.ds(d, w)
        inward[n]["far"].wait_recv()
        igp[planes, :, rows(z_of(way)), :] += zrel[planes]
        inward[n]["on"] = push(
            igp.at[planes, :, rows(z_of(way)), :], zrec.at[0, planes],
            in_sems, (n, 2), at_z(way),
        )

    def input_pair(n):
        d, w, way = INPUT_CHUNKS[n]
        planes = pl.ds(d, w)
        inward[n]["back"].wait_recv()
        inward[n]["on"].wait_recv()
        igp[planes, :, rows(gz), :] += zrec[0, planes] + zrec[1, planes]
        inward[n]["y"] = push(
            igp.at[planes, 1 - gy, rows(gz), :], yrec.at[planes], in_sems, (n, 3), at_y
        )

    def input_end(n):
        d, w, way = INPUT_CHUNKS[n]
        inward[n]["y"].wait_recv()
        for e in range(d, d + w):
            igv[:, e, :] = igp[e, gy, rows(gz), :] + yrec[e]

    wy_sems = (wy_s, wy_r)
    wx_sems = (wx_s, wx_r)
    weights = []

    def weight_start(n):
        t, w, way = TAP_CHUNKS[n]
        part_of = pl.ds(near + t, w)
        wsum[:, part_of] += w1b[:, t : t + w]
        weights.append(
            {
                "y": push(
                    wsum.at[:, part_of], wrel.at[:, pl.ds(t, w)], wy_sems, (n, 0),
                    next_y if way == 1 else prev_y,
                )
            }
        )

    def weight_relay(n):
        t, w, way = TAP_CHUNKS[n]
        weights[n]["y"].wait_recv()
        weights[n]["on"] = push(
            wrel.at[:, pl.ds(t, w)], warr.at[:, pl.ds(t, w)], wy_sems, (n, 1),
            next_y if way == 1 else prev_y,
        )

    scale = 1.0 / math.sqrt(PLANES * SLABS * PLANE)

    def weight_sum(n):
        t, w, way = TAP_CHUNKS[n]
        part_of = pl.ds(near + t, w)
        weights[n]["on"].wait_recv()
        wtot[:, t : t + w] = (wsum[:, part_of] + warr[:, t : t + w]) * scale
        for j in (2, 1, 3):
            weights[n]["x", j] = push(
                wtot.at[x_of(j), pl.ds(t, w)], wout.at[part_of, :, lanes(x)],
                wx_sems, (n, j - 1), at_x(j),
            )
        wout[part_of, :, lanes(x)] = wtot[x, t : t + w]

    def weight_swap(n):
        t, w, way = TAP_CHUNKS[n]
        for j in (1, 2, 3):
            weights[n]["x", j].wait_recv()
        here = wout.at[pl.ds(near + t, w)]
        weights[n]["mate"] = push(here, here, (w5_s, w5_r), n, (mate, f))

    input_start(0)
    first.wait_recv()
    for n in (0, 1, 2, 3):
        weight_start(n)
    input_start(1)
    rim_arrive()
    stack(0, 0)
    stack(PLANES + 1, 0)
    weight_relay(0)
    weight_relay(1)
    input_relay(0)
    input_start(2)
    weight_relay(2)
    weight_relay(3)
    input_relay(1)
    input_start(3)
    input_relay(2)
    weight_sum(0)
    weight_sum(1)
    input_pair(0)
    input_relay(3)
    input_pair(1)
    weight_sum(2)
    weight_sum(3)
    input_pair(2)
    weight_swap(0)
    weight_swap(1)
    input_end(0)
    input_end(1)
    input_pair(3)
    input_end(2)
    weight_swap(2)
    weight_swap(3)
    input_end(3)
    give_ig = pltpu.make_async_copy(igv, ig, local.at[1])
    give_ig.start()
    for n in range(4):
        weights[n]["mate"].wait_recv()
    give_wg = pltpu.make_async_copy(wout.at[pl.ds(0, TAPS)], wg, local.at[2])
    give_wg.start()

    for copy in sent:
        copy.wait_send()
    edge_leave()
    rim_leave()
    give_act.wait()
    give_ig.wait()
    give_wg.wait()


def scratch():
    I = ROWS * G
    O = ROWS * X
    H = PAD // 2
    columns = -(-TAPS * O // 128) * 128
    vmem = pltpu.VMEM
    dma = pltpu.SemaphoreType.DMA
    return [
        vmem((ROWS, PLANES, PLANE), F32),
        vmem((ROWS, PLANES, PLANE), F32),
        vmem((ROWS, PLANES, PLANE), F32),
        vmem((ROWS, PLANES, PLANE), F32),
        vmem((PLANES + 2, GY, GZ * ROWS, PLANE), F32),
        vmem((PLANES + 2, I, PLANE), BF16),
        vmem((PLANES + 2, I, PLANE), BF16),
        vmem((X, TAPS, ROWS, I), F32),
        vmem((9 * O, 3 * I), BF16),
        vmem((9 * O, 3 * I), BF16),
        vmem((columns, I), F32),
        vmem((I, columns), BF16),
        vmem((I, columns), BF16),
        vmem((9 * O, PLANE), F32),
        vmem((PLANES, O, PLANE), F32),
        vmem((X - 1, PLANES, ROWS, PLANE), F32),
        vmem((PLANES + 2, O, PLANE), F32),
        vmem((PLANES + 2, 9 * O, PLANE), BF16),
        vmem((PLANES + 2, 9 * O, PLANE), BF16),
        vmem((9 * O, 3 * I), F32),
        vmem((X, PAD, ROWS, I), F32),
        vmem((X, H, ROWS, I), F32),
        vmem((X, H, ROWS, I), F32),
        vmem((X, H, ROWS, I), F32),
        vmem((X, H, ROWS, I), F32),
        vmem((PAD, ROWS, X * I), F32),
        vmem((PLANES, GY, GZ * ROWS, PLANE), F32),
        vmem((PLANES, GY, ROWS, PLANE), F32),
        vmem((2, PLANES, GY, ROWS, PLANE), F32),
        vmem((PLANES, ROWS, PLANE), F32),
        dma((3,)),
        dma((4, 6)), dma((4, 6)),
        dma((6,)), dma((6,)),
        dma((2,)), dma((2,)),
        dma((4, 3)), dma((4, 3)),
        dma((4, 3)), dma((4, 3)),
        dma((2,)), dma((2,)),
        dma((4, 4)), dma((4, 4)),
        dma((1,)), dma((1,)),
        dma((4, 2)), dma((4, 2)),
        dma((4, 3)), dma((4, 3)),
        dma((4,)), dma((4,)),
    ]


def hand_out(act, ig, wg, act_out, ig_out, wg_out, sems):
    copies = [
        pltpu.make_async_copy(source, target, sems.at[n])
        for n, (source, target) in enumerate(((act, act_out), (ig, ig_out), (wg, wg_out)))
    ]
    for copy in copies:
        copy.start()
    for copy in copies:
        copy.wait()


def shards(volume, filters, out_grad):
    anywhere = pl.BlockSpec(memory_space=pl.ANY)
    shapes = (
        jax.ShapeDtypeStruct(volume.shape, F32),
        jax.ShapeDtypeStruct(volume.shape, F32),
        jax.ShapeDtypeStruct(filters.shape, F32),
    )
    held = pl.pallas_call(
        kernel,
        out_shape=shapes,
        in_specs=[anywhere] * 3,
        out_specs=(anywhere,) * 3,
        scratch_shapes=scratch(),
        compiler_params=pltpu.CompilerParams(
            collective_id=0, has_side_effects=True, vmem_limit_bytes=56 * 2**20
        ),
    )(volume, filters, out_grad)
    return pl.pallas_call(
        hand_out,
        out_shape=shapes,
        in_specs=[pl.BlockSpec(memory_space=pltpu.VMEM)] * 3,
        out_specs=(anywhere,) * 3,
        scratch_shapes=[pltpu.SemaphoreType.DMA((3,))],
    )(*held)


def solution(mesh):
    placed = (P("filt", "slab", None), P(None, "filt", None), P("filt", "slab", None))
    return jax.shard_map(
        shards,
        mesh=mesh,
        in_specs=placed,
        out_specs=(P("filt", "slab", None), P("filt", "slab", None), P(None, "filt", None)),
        check_vma=False,
    )
```

time: 76.5 us -> 66.6 us (0.87)
  Pallas kernels: 71.2 us -> 65.8 us
  local copies, waits for them, and re-layouts: 4.44 us -> 0 us
    pallas_call x1 -> x2, Pallas kernels: 71.2 us -> 65.8 us  [the longest x1 63.5 us: shards(): pl.pallas_call(kernel, out_shape=shapes, in_specs=[anywhere] * 3, out_spe...]
    unnamed x5 -> x0, local copies, waits for them, and re-layouts: 4.44 us -> none
where the time goes in v2:
time: 66.6 us; the launch traced here: 66.5 us
  Pallas kernels  65.8 us (99%)
    pallas_call x1, Pallas kernels, shards(): pl.pallas_call(kernel, out_shape=shapes, in_specs=[anywhere] * 3, out_spe...  63.5 us
    pallas_call x1, Pallas kernels, shards(): pl.pallas_call(hand_out, out_shape=shapes, in_specs=[pl.BlockSpec(memory_...  2.33 us

profile of v2, /device:TPU:1, one launch (start us, length us, event | category | flops | bytes accessed | tf_op | source)
XLA Modules:
  0.0 66.5 jit_solution(12121201427137036749)
XLA Ops:
  0.6 63.5 %shard_map.58 = (f32[16,8,256]{2,1,0:T(8,128)}, f32[16,8,256]{2,1,0:T(8,128)}, f32[27,16,512]{2,1,0:T(8,128)}) custom-call(f32[16,8,256]{2,1,0:T(8,128)} %vol.1, f32[27,16,512]{2,1,0:T(8,128)} %fil.1, f32[16,8,256]{2,1,0:T(8,128)} %og.1), custom_call_target="tpu_custom_call" | custom-call | tf_op jit(solution)/shard_map/pallas_call | solution.py:602
  64.2 2.3 %shard_map.59 = (f32[16,8,256]{2,1,0:T(8,128)}, f32[16,8,256]{2,1,0:T(8,128)}, f32[27,16,512]{2,1,0:T(8,128)}) custom-call(f32[16,8,256]{2,1,0:T(8,128)} %get-tuple-element.6.act, f32[16,8,256]{2,1,0:T(8,128)} %get-tuple-element.7.ig, f32[27,16,512]{2,1,0:T(8,128)} %get-tuple-element.8.wg), custom_call_target="tpu_custom_call" | custom-call | tf_op jit(solution)/shard_map/pallas_call | solution.py:612

commit v3 on v2

--- a/solution.py
+++ b/solution.py
@@ -18,9 +18,9 @@
 G = GY * GZ
 
 GATHER_CHUNKS = ((0, 2, 1), (6, 2, -1), (2, 2, 1), (4, 2, -1))
-REDUCE_CHUNKS = ((0, 2, 1), (2, 2, -1), (4, 2, 1), (6, 2, -1))
+REDUCE_CHUNKS = ((2, 2), (4, 2), (0, 2), (6, 2))
 INPUT_CHUNKS = ((2, 2, 1), (4, 2, -1), (0, 2, 1), (6, 2, -1))
-TAP_CHUNKS = ((0, 4, 1), (7, 4, -1), (4, 3, 1), (11, 3, -1))
+TAP_CHUNKS = ((0, 4), (4, 4), (8, 3), (11, 3))
 
 F32 = jnp.float32
 BF16 = jnp.bfloat16
@@ -33,17 +33,16 @@
 
 
 def product(left_high, left_low, right_high, right_low, dims):
-    def one(left, right):
-        return lax.dot_general(left, right, (dims, ((), ())), preferred_element_type=F32)
-
-    return one(left_high, right_high) + (one(left_high, right_low) + one(left_low, right_high))
+    left = jnp.concatenate([left_high, left_high, left_low], axis=dims[0][0])
+    right = jnp.concatenate([right_high, right_low, right_high], axis=dims[1][0])
+    return lax.dot_general(left, right, (dims, ((), ())), preferred_element_type=F32)
 
 
 def kernel(
     vol, fil, og, act, ig, wg,
     volv, ogv, actv, igv,
     g32, gh, gl, fa, w9h, w9l, wc, wth, wtl, taps, part, prec, pgx, sh, sl,
-    wacc, wsum, w1b, wrel, warr, wtot, wout, igp, zrel, zrec, yrec,
+    wacc, wsum, w1b, warr, wtot, wout, igp, zrel, zrec, yrec,
     local, g_s, g_r, fil_s, fil_r, hal_s, hal_r, rs_s, rs_r, ag_s, ag_r, ph_s, ph_r,
     in_s, in_r, w1_s, w1_r, wy_s, wy_r, wx_s, wx_r, w5_s, w5_r,
 ):
@@ -76,8 +75,6 @@
 
     flipped = x * G + (1 - gy) * GZ + gz
     at_y = (s, flipped)
-    next_y = (((half + gy) % 2) * 2 + core, flipped)
-    prev_y = (((half + 1 - gy) % 2) * 2 + core, flipped)
 
     def rows(index):
         return pl.ds(pl.multiple_of(index * ROWS, ROWS), ROWS)
@@ -88,7 +85,7 @@
     barrier = pltpu.get_barrier_semaphore()
     partners = [
         (mate, f), at_y, at_z(1), at_z(-1), at_x(1), at_x(-1), at_x(2), (other, f),
-        (across, flipped),
+        (across, f),
     ]
     for partner in partners:
         pl.semaphore_signal(
@@ -283,7 +280,7 @@
     reduce = []
 
     def reduce_start(n):
-        d, w, way = REDUCE_CHUNKS[n]
+        d, w = REDUCE_CHUNKS[n]
         planes = pl.ds(d, w)
         reduce.append(
             [
@@ -299,7 +296,7 @@
     spread = []
 
     def activate(n):
-        d, w, way = REDUCE_CHUNKS[n]
+        d, w = REDUCE_CHUNKS[n]
         for copy in reduce[n]:
             copy.wait_recv()
         for e in range(d, d + w):
@@ -310,10 +307,11 @@
         here = pgx.at[pl.ds(1 + d, w), rows(x), :]
         spread.append([push(here, here, ag_sems, (n, j - 1), at_x(j)) for j in (2, 1, 3)])
 
-    edge_arrive()
-    halve(0, 0)
-    halve(PLANES + 1, 0)
-    for n, (d, w, way) in enumerate(REDUCE_CHUNKS):
+    for n, (d, w) in enumerate(REDUCE_CHUNKS):
+        if n == 2:
+            edge_arrive()
+            halve(0, 0)
+            halve(PLANES + 1, 0)
         lax.fori_loop(d, d + w, forward, 0)
         reduce_start(n)
         if n == 1:
@@ -359,7 +357,7 @@
         return carry
 
     rim_start, rim_arrive, rim_leave = neighbours(pgx, ph_s, ph_r)
-    for n, (d, w, way) in enumerate(REDUCE_CHUNKS):
+    for n, (d, w) in enumerate(REDUCE_CHUNKS):
         for copy in spread[n]:
             copy.wait_recv()
         if n == 3:
@@ -437,32 +435,23 @@
     weights = []
 
     def weight_start(n):
-        t, w, way = TAP_CHUNKS[n]
+        t, w = TAP_CHUNKS[n]
         part_of = pl.ds(near + t, w)
         wsum[:, part_of] += w1b[:, t : t + w]
         weights.append(
             {
                 "y": push(
-                    wsum.at[:, part_of], wrel.at[:, pl.ds(t, w)], wy_sems, (n, 0),
-                    next_y if way == 1 else prev_y,
+                    wsum.at[:, part_of], warr.at[:, pl.ds(t, w)], wy_sems, n, (across, f)
                 )
             }
         )
 
-    def weight_relay(n):
-        t, w, way = TAP_CHUNKS[n]
+    scale = 1.0 / math.sqrt(PLANES * SLABS * PLANE)
+
+    def weight_sum(n):
+        t, w = TAP_CHUNKS[n]
+        part_of = pl.ds(near + t, w)
         weights[n]["y"].wait_recv()
-        weights[n]["on"] = push(
-            wrel.at[:, pl.ds(t, w)], warr.at[:, pl.ds(t, w)], wy_sems, (n, 1),
-            next_y if way == 1 else prev_y,
-        )
-
-    scale = 1.0 / math.sqrt(PLANES * SLABS * PLANE)
-
-    def weight_sum(n):
-        t, w, way = TAP_CHUNKS[n]
-        part_of = pl.ds(near + t, w)
-        weights[n]["on"].wait_recv()
         wtot[:, t : t + w] = (wsum[:, part_of] + warr[:, t : t + w]) * scale
         for j in (2, 1, 3):
             weights[n]["x", j] = push(
@@ -472,7 +461,7 @@
         wout[part_of, :, lanes(x)] = wtot[x, t : t + w]
 
     def weight_swap(n):
-        t, w, way = TAP_CHUNKS[n]
+        t, w = TAP_CHUNKS[n]
         for j in (1, 2, 3):
             weights[n]["x", j].wait_recv()
         here = wout.at[pl.ds(near + t, w)]
@@ -486,12 +475,8 @@
     rim_arrive()
     stack(0, 0)
     stack(PLANES + 1, 0)
-    weight_relay(0)
-    weight_relay(1)
     input_relay(0)
     input_start(2)
-    weight_relay(2)
-    weight_relay(3)
     input_relay(1)
     input_start(3)
     input_relay(2)
@@ -560,14 +545,13 @@
         vmem((X, H, ROWS, I), F32),
         vmem((X, H, ROWS, I), F32),
         vmem((X, H, ROWS, I), F32),
-        vmem((X, H, ROWS, I), F32),
         vmem((PAD, ROWS, X * I), F32),
         vmem((PLANES, GY, GZ * ROWS, PLANE), F32),
         vmem((PLANES, GY, ROWS, PLANE), F32),
         vmem((2, PLANES, GY, ROWS, PLANE), F32),
         vmem((PLANES, ROWS, PLANE), F32),
         dma((3,)),
-        dma((4, 6)), dma((4, 6)),
+        dma((len(GATHER_CHUNKS), 6)), dma((len(GATHER_CHUNKS), 6)),
         dma((6,)), dma((6,)),
         dma((2,)), dma((2,)),
         dma((4, 3)), dma((4, 3)),
@@ -575,7 +559,7 @@
         dma((2,)), dma((2,)),
         dma((4, 4)), dma((4, 4)),
         dma((1,)), dma((1,)),
-        dma((4, 2)), dma((4, 2)),
+        dma((4,)), dma((4,)),
         dma((4, 3)), dma((4, 3)),
         dma((4,)), dma((4,)),
     ]

time: 66.6 us -> 62.3 us (0.935)
  Pallas kernels: 65.8 us -> 61.5 us
    pallas_call x1, Pallas kernels: 63.5 us -> 59.2 us  [shards(): pl.pallas_call(kernel, out_shape=shapes, in_specs=[anywhere] * 3, out_spe...]
where the time goes in v3:
time: 62.3 us; the launch traced here: 62.1 us
  Pallas kernels  61.5 us (99%)
  between operations  0.64 us (1%)
    pallas_call x1, Pallas kernels, shards(): pl.pallas_call(kernel, out_shape=shapes, in_specs=[anywhere] * 3, out_spe...  59.2 us
    pallas_call x1, Pallas kernels, shards(): pl.pallas_call(hand_out, out_shape=shapes, in_specs=[pl.BlockSpec(memory_...  2.33 us

profile of v3, /device:TPU:1, one launch (start us, length us, event | category | flops | bytes accessed | tf_op | source)
XLA Modules:
  0.0 62.1 jit_solution(16880511123160753441)
XLA Ops:
  0.6 59.2 %shard_map.58 = (f32[16,8,256]{2,1,0:T(8,128)}, f32[16,8,256]{2,1,0:T(8,128)}, f32[27,16,512]{2,1,0:T(8,128)}) custom-call(f32[16,8,256]{2,1,0:T(8,128)} %vol.1, f32[27,16,512]{2,1,0:T(8,128)} %fil.1, f32[16,8,256]{2,1,0:T(8,128)} %og.1), custom_call_target="tpu_custom_call" | custom-call | tf_op jit(solution)/shard_map/pallas_call | solution.py:586
  59.8 2.3 %shard_map.59 = (f32[16,8,256]{2,1,0:T(8,128)}, f32[16,8,256]{2,1,0:T(8,128)}, f32[27,16,512]{2,1,0:T(8,128)}) custom-call(f32[16,8,256]{2,1,0:T(8,128)} %get-tuple-element.6.act, f32[16,8,256]{2,1,0:T(8,128)} %get-tuple-element.7.ig, f32[27,16,512]{2,1,0:T(8,128)} %get-tuple-element.8.wg), custom_call_target="tpu_custom_call" | custom-call | tf_op jit(solution)/shard_map/pallas_call | solution.py:596

commit v4 on v3

--- a/solution.py
+++ b/solution.py
@@ -499,18 +499,21 @@
     input_end(3)
     give_ig = pltpu.make_async_copy(igv, ig, local.at[1])
     give_ig.start()
-    for n in range(4):
+    gifts = [give_act, give_ig]
+    for n, (t, w) in enumerate(TAP_CHUNKS):
         weights[n]["mate"].wait_recv()
-    give_wg = pltpu.make_async_copy(wout.at[pl.ds(0, TAPS)], wg, local.at[2])
-    give_wg.start()
+        for k in range(2):
+            taps_of = pl.ds(k * H + t, min(w, TAPS - k * H - t))
+            give = pltpu.make_async_copy(wout.at[taps_of], wg.at[taps_of], local.at[2 + 2 * n + k])
+            give.start()
+            gifts.append(give)
 
     for copy in sent:
         copy.wait_send()
     edge_leave()
     rim_leave()
-    give_act.wait()
-    give_ig.wait()
-    give_wg.wait()
+    for give in gifts:
+        give.wait()
 
 
 def scratch():
@@ -550,7 +553,7 @@
         vmem((PLANES, GY, ROWS, PLANE), F32),
         vmem((2, PLANES, GY, ROWS, PLANE), F32),
         vmem((PLANES, ROWS, PLANE), F32),
-        dma((3,)),
+        dma((10,)),
         dma((len(GATHER_CHUNKS), 6)), dma((len(GATHER_CHUNKS), 6)),
         dma((6,)), dma((6,)),
         dma((2,)), dma((2,)),
@@ -565,14 +568,20 @@
     ]
 
 
-def hand_out(act, ig, wg, act_out, ig_out, wg_out, sems):
-    copies = [
-        pltpu.make_async_copy(source, target, sems.at[n])
-        for n, (source, target) in enumerate(((act, act_out), (ig, ig_out), (wg, wg_out)))
-    ]
-    for copy in copies:
+def hand_out(act, ig, wg, act_out, ig_out, wg_out, act_held, ig_held, wg_held, into, out):
+    parts = [(act, act_held, act_out), (ig, ig_held, ig_out)]
+    third = TAPS // 3
+    for n in range(3):
+        part = pl.ds(n * third, third)
+        parts.append((wg.at[part], wg_held.at[part], wg_out.at[part]))
+    bring = [pltpu.make_async_copy(p[0], p[1], into.at[n]) for n, p in enumerate(parts)]
+    give = [pltpu.make_async_copy(p[1], p[2], out.at[n]) for n, p in enumerate(parts)]
+    for copy in bring:
         copy.start()
-    for copy in copies:
+    for first, second in zip(bring, give):
+        first.wait()
+        second.start()
+    for copy in give:
         copy.wait()
 
 
@@ -596,9 +605,12 @@
     return pl.pallas_call(
         hand_out,
         out_shape=shapes,
-        in_specs=[pl.BlockSpec(memory_space=pltpu.VMEM)] * 3,
+        in_specs=[anywhere] * 3,
         out_specs=(anywhere,) * 3,
-        scratch_shapes=[pltpu.SemaphoreType.DMA((3,))],
+        scratch_shapes=[
+            *(pltpu.VMEM(shape.shape, F32) for shape in shapes),
+            pltpu.SemaphoreType.DMA((5,)), pltpu.SemaphoreType.DMA((5,)),
+        ],
     )(*held)
 
 

time: 62.3 us -> 61.8 us (level)
  no operation moved by 1% of the time
where the time goes in v4:
time: 61.8 us; the launch traced here: 61.7 us
  Pallas kernels  61.1 us (99%)
  between operations  0.64 us (1%)
    pallas_call x1, Pallas kernels, shards(): pl.pallas_call(kernel, out_shape=shapes, in_specs=[anywhere] * 3, out_spe...  59 us
    pallas_call x1, Pallas kernels, shards(): pl.pallas_call(hand_out, out_shape=shapes, in_specs=[anywhere] * 3, out_s...  2.09 us

profile of v4, /device:TPU:1, one launch (start us, length us, event | category | flops | bytes accessed | tf_op | source)
XLA Modules:
  0.0 61.7 jit_solution(14641270073611581519)
XLA Ops:
  0.6 59.0 %shard_map.58 = (f32[16,8,256]{2,1,0:T(8,128)}, f32[16,8,256]{2,1,0:T(8,128)}, f32[27,16,512]{2,1,0:T(8,128)}) custom-call(f32[16,8,256]{2,1,0:T(8,128)} %vol.1, f32[27,16,512]{2,1,0:T(8,128)} %fil.1, f32[16,8,256]{2,1,0:T(8,128)} %og.1), custom_call_target="tpu_custom_call" | custom-call | tf_op jit(solution)/shard_map/pallas_call | solution.py:595
  59.6 2.1 %shard_map.59 = (f32[16,8,256]{2,1,0:T(8,128)}, f32[16,8,256]{2,1,0:T(8,128)}, f32[27,16,512]{2,1,0:T(8,128)}) custom-call(f32[16,8,256]{2,1,0:T(8,128)} %get-tuple-element.6.act, f32[16,8,256]{2,1,0:T(8,128)} %get-tuple-element.7.ig, f32[27,16,512]{2,1,0:T(8,128)} %get-tuple-element.8.wg), custom_call_target="tpu_custom_call" | custom-call | tf_op jit(solution)/shard_map/pallas_call | solution.py:605

commit v5 on v4

--- a/solution.py
+++ b/solution.py
@@ -41,7 +41,7 @@
 def kernel(
     vol, fil, og, act, ig, wg,
     volv, ogv, actv, igv,
-    g32, gh, gl, fa, w9h, w9l, wc, wth, wtl, taps, part, prec, pgx, sh, sl,
+    g32, gh, gl, fa, w9h, w9l, wc, wt, taps, part, prec, pgx, sh, sl,
     wacc, wsum, w1b, warr, wtot, wout, igp, zrel, zrec, yrec,
     local, g_s, g_r, fil_s, fil_r, hal_s, hal_r, rs_s, rs_r, ag_s, ag_r, ph_s, ph_r,
     in_s, in_r, w1_s, w1_r, wy_s, wy_r, wx_s, wx_r, w5_s, w5_r,
@@ -190,8 +190,8 @@
     def transpose(n, carry):
         start = pl.multiple_of(n * 128, 128)
         high, low = split(wc[pl.ds(start, 128), :].T)
-        wth[:, pl.ds(start, 128)] = high
-        wtl[:, pl.ds(start, 128)] = low
+        wt[:I, pl.ds(start, 128)] = high
+        wt[I:, pl.ds(start, 128)] = low
         return carry
 
     def neighbours(buffer, send, recv):
@@ -346,15 +346,18 @@
                 sl[e, k * O : (k + 1) * O, :] = low
         return carry
 
-    def weigh(d, carry):
-        stack(d + 1, 0)
-        term = product(
-            sh[d + 1], sl[d + 1],
-            gh[pl.ds(d, 3)].reshape(3 * I, PLANE), gl[pl.ds(d, 3)].reshape(3 * I, PLANE),
-            ((1,), (1,)),
-        )
-        wacc[...] += term
-        return carry
+    def weigh(d, w):
+        lax.fori_loop(d + 1, d + 1 + w, stack, 0)
+
+        def fields(stacked):
+            return jnp.concatenate([stacked[e] for e in range(d + 1, d + 1 + w)], axis=1)
+
+        def inputs(held):
+            return jnp.concatenate(
+                [held[e : e + 3].reshape(3 * I, PLANE) for e in range(d, d + w)], axis=1
+            )
+
+        wacc[...] += product(fields(sh), fields(sl), inputs(gh), inputs(gl), ((1,), (1,)))
 
     rim_start, rim_arrive, rim_leave = neighbours(pgx, ph_s, ph_r)
     for n, (d, w) in enumerate(REDUCE_CHUNKS):
@@ -363,7 +366,7 @@
         if n == 3:
             rim_start()
             leaves.append(rim_leave)
-        lax.fori_loop(d, d + w, weigh, 0)
+        weigh(d, w)
 
     for a in range(3):
         for k in range(9):
@@ -376,11 +379,15 @@
     )
 
     def backward(d, carry):
-        value = product(
-            wth[:, : TAPS * O], wtl[:, : TAPS * O],
-            sh[pl.ds(d, 3)].reshape(TAPS * O, PLANE), sl[pl.ds(d, 3)].reshape(TAPS * O, PLANE),
-            ((1,), (0,)),
-        )
+        high = jnp.dot(
+            wt[:, : TAPS * O], sh[pl.ds(d, 3)].reshape(TAPS * O, PLANE),
+            preferred_element_type=F32,
+        )
+        low = jnp.dot(
+            wt[:I, : TAPS * O], sl[pl.ds(d, 3)].reshape(TAPS * O, PLANE),
+            preferred_element_type=F32,
+        )
+        value = high[:I] + (high[I:] + low)
         igp[d] = value.reshape(GY, GZ * ROWS, PLANE)
         return carry
 
@@ -535,8 +542,7 @@
         vmem((9 * O, 3 * I), BF16),
         vmem((9 * O, 3 * I), BF16),
         vmem((columns, I), F32),
-        vmem((I, columns), BF16),
-        vmem((I, columns), BF16),
+        vmem((2 * I, columns), BF16),
         vmem((9 * O, PLANE), F32),
         vmem((PLANES, O, PLANE), F32),
         vmem((X - 1, PLANES, ROWS, PLANE), F32),

time: 61.8 us -> 61.8 us (level)
  no operation moved by 1% of the time
where the time goes in v5:
time: 61.8 us; the launch traced here: 61.7 us
  Pallas kernels  61 us (99%)
  between operations  0.64 us (1%)
    pallas_call x1, Pallas kernels, shards(): pl.pallas_call(kernel, out_shape=shapes, in_specs=[anywhere] * 3, out_spe...  59 us
    pallas_call x1, Pallas kernels, shards(): pl.pallas_call(hand_out, out_shape=shapes, in_specs=[anywhere] * 3, out_s...  2.09 us

profile of v5, /device:TPU:1, one launch (start us, length us, event | category | flops | bytes accessed | tf_op | source)
XLA Modules:
  0.0 61.7 jit_solution(15152230861616525402)
XLA Ops:
  0.6 59.0 %shard_map.58 = (f32[16,8,256]{2,1,0:T(8,128)}, f32[16,8,256]{2,1,0:T(8,128)}, f32[27,16,512]{2,1,0:T(8,128)}) custom-call(f32[16,8,256]{2,1,0:T(8,128)} %vol.1, f32[27,16,512]{2,1,0:T(8,128)} %fil.1, f32[16,8,256]{2,1,0:T(8,128)} %og.1), custom_call_target="tpu_custom_call" | custom-call | tf_op jit(solution)/shard_map/pallas_call | solution.py:601
  59.6 2.1 %shard_map.59 = (f32[16,8,256]{2,1,0:T(8,128)}, f32[16,8,256]{2,1,0:T(8,128)}, f32[27,16,512]{2,1,0:T(8,128)}) custom-call(f32[16,8,256]{2,1,0:T(8,128)} %get-tuple-element.6.act, f32[16,8,256]{2,1,0:T(8,128)} %get-tuple-element.7.ig, f32[27,16,512]{2,1,0:T(8,128)} %get-tuple-element.8.wg), custom_call_target="tpu_custom_call" | custom-call | tf_op jit(solution)/shard_map/pallas_call | solution.py:611

commit v6 on v5

--- a/solution.py
+++ b/solution.py
@@ -138,16 +138,6 @@
 
     strip = pl.ds(pl.multiple_of(core * (ROWS // 2), ROWS // 2), ROWS // 2)
     fil_sems = (fil_s, fil_r)
-    filters = []
-    for j in (1, 3, 2):
-        filters.append(
-            (
-                x_of(-j),
-                push(
-                    fil.at[:, strip, lanes(x_of(j))], fa.at[x, :, strip], fil_sems, j - 1, at_x(j)
-                ),
-            )
-        )
     g_sems = (g_s, g_r)
     gather = []
     for n, (d, w, way) in enumerate(GATHER_CHUNKS):
@@ -158,6 +148,16 @@
                 ("own", 1): push(here, here, g_sems, (n, 1), at_z(1)),
                 ("own", -1): push(here, here, g_sems, (n, 2), at_z(-1)),
             }
+        )
+    filters = []
+    for j in (1, 3, 2):
+        filters.append(
+            (
+                x_of(-j),
+                push(
+                    fil.at[:, strip, lanes(x_of(j))], fa.at[x, :, strip], fil_sems, j - 1, at_x(j)
+                ),
+            )
         )
     for n, (d, w, way) in enumerate(GATHER_CHUNKS):
         gather[n]["y"].wait_recv()

time: 61.8 us -> 61.8 us (level)
  no operation moved by 1% of the time
where the time goes in v6:
time: 61.8 us; the launch traced here: 61.7 us
  Pallas kernels  61.1 us (99%)
  between operations  0.64 us (1%)
    pallas_call x1, Pallas kernels, shards(): pl.pallas_call(kernel, out_shape=shapes, in_specs=[anywhere] * 3, out_spe...  59 us
    pallas_call x1, Pallas kernels, shards(): pl.pallas_call(hand_out, out_shape=shapes, in_specs=[anywhere] * 3, out_s...  2.09 us

profile of v6, /device:TPU:1, one launch (start us, length us, event | category | flops | bytes accessed | tf_op | source)
XLA Modules:
  0.0 61.7 jit_solution(14128380252521854109)
XLA Ops:
  0.6 59.0 %shard_map.58 = (f32[16,8,256]{2,1,0:T(8,128)}, f32[16,8,256]{2,1,0:T(8,128)}, f32[27,16,512]{2,1,0:T(8,128)}) custom-call(f32[16,8,256]{2,1,0:T(8,128)} %vol.1, f32[27,16,512]{2,1,0:T(8,128)} %fil.1, f32[16,8,256]{2,1,0:T(8,128)} %og.1), custom_call_target="tpu_custom_call" | custom-call | tf_op jit(solution)/shard_map/pallas_call | solution.py:601
  59.6 2.1 %shard_map.59 = (f32[16,8,256]{2,1,0:T(8,128)}, f32[16,8,256]{2,1,0:T(8,128)}, f32[27,16,512]{2,1,0:T(8,128)}) custom-call(f32[16,8,256]{2,1,0:T(8,128)} %get-tuple-element.6.act, f32[16,8,256]{2,1,0:T(8,128)} %get-tuple-element.7.ig, f32[27,16,512]{2,1,0:T(8,128)} %get-tuple-element.8.wg), custom_call_target="tpu_custom_call" | custom-call | tf_op jit(solution)/shard_map/pallas_call | solution.py:611
